TPU v7x, 512 devices: a whole 4x4x16 slice. The times are simulated.
512 devices in a mesh: particle: 16 (over y, x), seq: 32 (over z, core).
Axes of the slice: x: 4, y: 4, z: 16, core: 2. Of those that a mesh axis runs over, the one named last changes fastest.
Arguments:
- latents: bfloat16 [32, 4096, 1536], P('particle', 'seq'), may hold values from -6 to 6
- mod_table: float32 [28, 3072], replicated, may hold values from -3 to 3
- step_index: int32 [1], replicated, may hold values from 0 to 27
- qkv_weight: bfloat16 [1536, 3072], P(('particle', 'seq')), may hold values from -0.15625 to 0.15625
- text_kv: bfloat16 [64, 154, 128], replicated, may hold values from -400 to 400
- ancestors: int32 [32], replicated, may hold values from 0 to 31, as said below
Outputs:
- attended: bfloat16 [32, 4096, 1024], P('particle', 'seq')
Inputs may be any that keep to these rules, and one draw needn't show every extreme that they name: ancestors[d] lies in the same block of 8 consecutive particles as d; within each block the ancestors do not decrease, and the block's first and last particles are their own ancestors.
All inputs are finite; a program needn't handle non-finite values.
Results may differ from a plain program's by a relative error of at most 0.0059.
The roundings to bfloat16 on the way count: a program that leaves them out, or rounds other values in their place, can miss the bound.
Values may be sent and summed in bfloat16 or wider, within the bound.
A program may use at most 128 MiB of HBM per device.

v0:
```python
import jax
import jax.numpy as jnp
from jax import lax
from jax.sharding import PartitionSpec as P

HEADS = 16
HD = 64
PER_PROMPT = 8


def shifted(value, axis, steps):
    count = lax.axis_size(axis)
    initial, last = (max(0, -steps), min(count, count - steps))
    return lax.ppermute(value, axis, [(source, source + steps) for source in range(initial, last)])


def modulate(rows, shift, scale):
    values = rows.astype(jnp.float32)
    mean = jnp.mean(values, axis=-1, keepdims=True)
    centred = values - mean
    var = jnp.mean(centred * centred, axis=-1, keepdims=True)
    normed = centred / jnp.sqrt(var + 1e-06)
    return (normed * (1.0 + scale) + shift).astype(jnp.bfloat16)


def resample(field, ancestors):
    part_dev = field.shape[0]
    group = lax.axis_index("particle")
    span = max(PER_PROMPT // part_dev, 1)
    mine = lax.dynamic_slice_in_dim(ancestors, group * part_dev, part_dev, 0)
    offset = group - mine // part_dev
    local_index = mine % part_dev
    result = jnp.zeros_like(field)
    for step_by in range(-(span - 1), span):
        if step_by == 0:
            piece = field
        else:
            piece = shifted(field, "particle", step_by)
        chosen = jnp.take(piece, local_index, axis=0)
        keep = (offset == step_by).reshape((part_dev,) + (1,) * (field.ndim - 1))
        result = jnp.where(keep, chosen, result)
    return result


def block_attend(query, keys, values):
    scores = jnp.dot(query, keys.T, preferred_element_type=jnp.float32) * HD ** (-0.5)
    expo = jnp.exp(scores - jnp.max(scores, axis=-1, keepdims=True))
    total = jnp.sum(expo, axis=-1, keepdims=True)
    mixed = jnp.dot(expo.astype(jnp.bfloat16), values, preferred_element_type=jnp.float32)
    return (mixed / total).astype(jnp.bfloat16)


def attend_item(pair):
    item_qkv, item_text = pair
    length = item_qkv.shape[0]
    keys = jnp.concatenate([item_qkv[:, HD : 2 * HD], item_text[:, 0:HD]], axis=0)
    values = jnp.concatenate([item_qkv[:, 2 * HD : 3 * HD], item_text[:, HD : 2 * HD]], axis=0)
    block_rows = min(512, length)
    queries = item_qkv[:, 0:HD].reshape(length // block_rows, block_rows, HD)
    outputs = lax.map(lambda query: block_attend(query, keys, values), queries)
    return outputs.reshape(length, HD)


def local(latents, mod_table, step_index, qkv_weight, text_kv, ancestors):
    part_dev, rows, width = latents.shape
    select = (jnp.arange(mod_table.shape[0], dtype=jnp.int32) == step_index[0]).astype(jnp.float32)
    modrow = jnp.sum(mod_table * select[:, None], axis=0)
    shift = modrow[0:width]
    scale = modrow[width : 2 * width]
    states = resample(latents, ancestors)
    modded = modulate(states, shift, scale).reshape(part_dev * rows, width)
    projected = jnp.dot(
        modded,
        lax.all_gather(qkv_weight, ("particle", "seq"), axis=0, tiled=True),
        preferred_element_type=jnp.float32,
    )
    qkv = projected.astype(jnp.bfloat16).reshape(part_dev, rows, HEADS, 3 * HD)
    qkv = qkv.transpose(0, 2, 1, 3).reshape(part_dev * HEADS, rows, 3 * HD)
    per_item = lax.all_to_all(qkv, "seq", split_axis=0, concat_axis=1, tiled=True)
    count = per_item.shape[0]
    items = lax.axis_index("seq") * count + jnp.arange(count, dtype=jnp.int32)
    owner = lax.axis_index("particle") * part_dev + items // HEADS
    text_rows = owner // PER_PROMPT * HEADS + items % HEADS
    texts = jnp.take(text_kv, text_rows, axis=0)
    attended = lax.map(attend_item, (per_item, texts))
    returned = lax.all_to_all(attended, "seq", split_axis=1, concat_axis=0, tiled=True)
    returned = returned.reshape(part_dev, HEADS, rows, HD).transpose(0, 2, 1, 3)
    result = returned.reshape(part_dev, rows, HEADS * HD)
    return result


def solution(mesh):
    in_specs = (P("particle", "seq", None), P(), P(), P(("particle", "seq"), None), P(), P())
    out_specs = P("particle", "seq", None)
    return jax.shard_map(local, mesh=mesh, in_specs=in_specs, out_specs=out_specs, check_vma=False)
```

profile of v0, /device:TPU:1, one launch (start us, length us, event | category | flops | bytes accessed | tf_op | source)
XLA Modules:
  0.0 515.2 jit_solution(8882409692523677508)
XLA Ops:
  7.3 1.4 collective-permute-start.3
  8.7 5.5 %collective-permute-start.2 = (bf16[2,128,1536]{2,1,0:T(8,128)(2,1)}, bf16[2,128,1536]{2,1,0:T(8,128)(2,1)}, u32[]{:S(2)}, u32[]{:S(2)}) collective-permute-start(bf16[2,128,1536]{2,1,0:T(8,128)(2,1)} %param.10), channel_id=1, source_target_pairs={{0,32},{32,64},{64,96},{96,128},{128,160},{160,192},{192,224},{224... | collective-permute-start | bytes 2359304 | tf_op jit(solution)/shard_map/ppermute | solution.py:14
  14.2 4.9 collective-permute-start.1
  19.1 3.7 collective-permute-start
  26.9 1.7 gather_fusion.3
  29.8 2.6 gather_fusion.4
  32.4 2.6 gather_fusion.2
  35.0 5.8 %collective-permute-done.1 = bf16[2,128,1536]{2,1,0:T(8,128)(2,1)} collective-permute-done((bf16[2,128,1536]{2,1,0:T(8,128)(2,1)}, bf16[2,128,1536]{2,1,0:T(8,128)(2,1)}, u32[]{:S(2)}, u32[]{:S(2)}) %collective-permute-start.1) | collective-permute-done | bytes 786464 | tf_op jit(solution)/shard_map/ppermute | solution.py:14
  40.8 2.6 gather_fusion.1
  43.4 10.2 %collective-permute-done = bf16[2,128,1536]{2,1,0:T(8,128)(2,1)} collective-permute-done((bf16[2,128,1536]{2,1,0:T(8,128)(2,1)}, bf16[2,128,1536]{2,1,0:T(8,128)(2,1)}, u32[]{:S(2)}, u32[]{:S(2)}) %collective-permute-start) | collective-permute-done | bytes 786464 | tf_op jit(solution)/shard_map/ppermute | solution.py:14
  53.7 2.6 gather_fusion
  56.3 34.2 %collective-permute-done.5 = bf16[2,128,1536]{2,1,0:T(8,128)(2,1)} collective-permute-done((bf16[2,128,1536]{2,1,0:T(8,128)(2,1)}, bf16[2,128,1536]{2,1,0:T(8,128)(2,1)}, u32[]{:S(2)}, u32[]{:S(2)}) %collective-permute-start.5) | collective-permute-done | bytes 786464 | tf_op jit(solution)/shard_map/ppermute | solution.py:14
  90.5 2.6 gather_fusion.6
  93.1 2.7 gather_fusion.5
  95.8 3.6 convert_reduce_fusion
  100.2 161.1 %all-gather.3.cloned.1.call-done = bf16[512,3,3072]{2,1,0:T(4,128)(2,1)} async-done(((bf16[1,3,3072]{2,1,0:T(4,128)(2,1)}), bf16[512,3,3072]{2,1,0:T(4,128)(2,1)}) %all-gather.3.cloned.1.call-update) | async-done | bytes 9437200 | tf_op jit(solution)/shard_map/all_gather | solution.py:74
  261.3 23.5 %reshape.185 = bf16[1536,3072]{1,0:T(8,128)(2,1)} reshape(bf16[512,3,3072]{2,1,0:T(4,128)(2,1)} %all-gather.3.cloned.1.call-done) | data formatting | bytes 18874368
  284.7 7.4 %convolution_convert_fusion = bf16[256,3072]{1,0:T(8,128)(2,1)} fusion(bf16[256,1536]{1,0:T(8,128)(2,1)S(1)} %bitcast.60, bf16[1536,3072]{1,0:T(8,128)(2,1)} %reshape.185), kind=kOutput, calls=%fused_computation.20 | convolution fusion | flops 2416705536 | bytes 11796480 | tf_op jit(solution)/shard_map/dot_general | solution.py:72
  292.1 2.6 copy.24
  294.7 3.5 reshape.88
  298.2 2.9 copy.25
  301.1 8.2 %all-to-all-start = ((bf16[32,128,192]{1,2,0:T(8,128)(2,1)}), bf16[32,128,192]{1,2,0:T(8,128)(2,1)}, u32[]{:S(2)}, u32[]{:S(2)}) async-start(bf16[32,128,192]{1,2,0:T(8,128)(2,1)} %bitcast.54), calls=%async_computation | async-start | bytes 3145728 | tf_op jit(solution)/shard_map/all_to_all | solution.py:79
  309.7 77.7 %all-to-all-done = bf16[32,128,192]{1,2,0:T(8,128)(2,1)} async-done(((bf16[32,128,192]{1,2,0:T(8,128)(2,1)}), bf16[32,128,192]{1,2,0:T(8,128)(2,1)}, u32[]{:S(2)}, u32[]{:S(2)}) %all-to-all-start) | async-done | bytes 1572896 | tf_op jit(solution)/shard_map/all_to_all | solution.py:79
  387.4 1.6 copy_bitcast_fusion
  391.9 2.4 copy.36
  394.3 38.5 %while.18 = (s32[]{:T(128)}, bf16[8,512,64]{1,2,0:T(8,128)(2,1)S(1)}, bf16[8,512,64]{2,1,0:T(8,128)(2,1)}, bf16[4250,64]{1,0:T(8,128)(2,1)S(1)}, bf16[4250,64]{1,0:T(8,128)(2,1)S(1)}, /*index=5*/s32[]{:T(128)}) while((s32[]{:T(128)}, bf16[8,512,64]{1,2,0:T(8,128)(2,1)S(1)}, bf16[8,512,64]{2,1,0:T(8,128)(2,1)}, bf16[4250,64]{1,0:T(8,128)(2,1)S(1)}, ...), condition=%wide.region_6.8_spmd, body=%wide.region_3.7_spmd.sunk | while | flops 570176512 | bytes 27964756 | solution.py:60
  394.3 2.2 fusion.52
  397.8 1.4 fusion.54
  399.2 2.2 fusion.52
  402.6 1.4 fusion.54
  404.0 2.2 fusion.52
  407.4 1.4 fusion.54
  408.8 2.2 fusion.52
  412.3 1.4 fusion.54
  413.6 2.2 fusion.52
  417.1 1.3 fusion.54
  418.4 2.2 fusion.52
  421.9 1.4 fusion.54
  423.3 2.2 fusion.52
  426.7 1.3 fusion.54
  428.1 2.2 fusion.52
  431.5 1.4 fusion.54
  432.9 1.3 copy.37
  434.2 5.8 %reshape.200 = bf16[1,4096,64]{2,0,1:T(2,128)(2,1)S(1)} reshape(bf16[8,512,64]{2,1,0:T(8,128)(2,1)} %copy.37) | data formatting | bytes 1048576 | tf_op jit(solution)/shard_map/while/body/jit(dynamic_update_index_in_dim)/broadcast_in_dim | solution.py:85
  440.5 23.4 %reduce = bf16[4096,64]{1,0:T(8,128)(2,1)} reduce(bf16[4096,1,64]{2,1,0:T(2,128)(2,1)S(1)} %bitcast.53, bf16[]{:T(256)} %broadcast.203), dimensions={1}, to_apply=%bitcast.33.reduce_sub_computation | reduce | bytes 1048578
  463.9 2.3 reshape.201
  466.3 36.7 %all_to_all.8 = bf16[32,2,4096]{2,1,0:T(2,128)(2,1)S(1)} all-to-all(bf16[32,2,4096]{2,1,0:T(2,128)(2,1)S(1)} %reshape.201), channel_id=1, replica_groups=mesh['particle'=16,'seq'=32] {'seq'}, dimensions={0} | all-to-all | bytes 1048576 | tf_op jit(solution)/shard_map/all_to_all | solution.py:86
  504.2 2.3 copy.33
  (48 shorter events, 22.4 us)
Async XLA Ops:
  6.5 302.9 %copy-start = (bf16[64,154,128]{2,0,1:T(8,128)(2,1)S(1)}, bf16[64,154,128]{2,0,1:T(8,128)(2,1)}, u32[]{:S(2)}) copy-start(bf16[64,154,128]{2,0,1:T(8,128)(2,1)} %param.14) | copy-start | bytes 7569412
  6.5 254.7 %all-gather.3.cloned.1.call-start = ((), (), s32[]{:S(2)}) async-start(), calls=%async_computation.2 | async-start | bytes 12607488 | tf_op jit(solution)/shard_map/all_gather | solution.py:74
  7.3 18.3 %collective-permute-start.3 = (bf16[2,128,1536]{2,1,0:T(8,128)(2,1)}, bf16[2,128,1536]{2,1,0:T(8,128)(2,1)S(1)}, u32[]{:S(2)}, u32[]{:S(2)}) collective-permute-start(bf16[2,128,1536]{2,1,0:T(8,128)(2,1)} %param.10), channel_id=1, source_target_pairs={{32,0},{64,32},{96,64},{128,96},{160,128},{192,160},{224,192},{256... | collective-permute-start | bytes 2359304 | tf_op jit(solution)/shard_map/ppermute | solution.py:14
  8.7 23.7 %collective-permute-start.2 = (bf16[2,128,1536]{2,1,0:T(8,128)(2,1)}, bf16[2,128,1536]{2,1,0:T(8,128)(2,1)}, u32[]{:S(2)}, u32[]{:S(2)}) collective-permute-start(bf16[2,128,1536]{2,1,0:T(8,128)(2,1)} %param.10), channel_id=1, source_target_pairs={{0,32},{32,64},{64,96},{96,128},{128,160},{160,192},{192,224},{224... | collective-permute-start | bytes 2359304 | tf_op jit(solution)/shard_map/ppermute | solution.py:14
  14.2 26.6 %collective-permute-start.1 = (bf16[2,128,1536]{2,1,0:T(8,128)(2,1)}, bf16[2,128,1536]{2,1,0:T(8,128)(2,1)}, u32[]{:S(2)}, u32[]{:S(2)}) collective-permute-start(bf16[2,128,1536]{2,1,0:T(8,128)(2,1)} %param.10), channel_id=1, source_target_pairs={{0,64},{32,96},{64,128},{96,160},{128,192},{160,224},{192,256},{22... | collective-permute-start | bytes 2359304 | tf_op jit(solution)/shard_map/ppermute | solution.py:14
  19.1 34.6 %collective-permute-start = (bf16[2,128,1536]{2,1,0:T(8,128)(2,1)}, bf16[2,128,1536]{2,1,0:T(8,128)(2,1)}, u32[]{:S(2)}, u32[]{:S(2)}) collective-permute-start(bf16[2,128,1536]{2,1,0:T(8,128)(2,1)} %param.10), channel_id=1, source_target_pairs={{0,96},{32,128},{64,160},{96,192},{128,224},{160,256},{192,288},{2... | collective-permute-start | bytes 2359304 | tf_op jit(solution)/shard_map/ppermute | solution.py:14
  22.8 67.7 %collective-permute-start.5 = (bf16[2,128,1536]{2,1,0:T(8,128)(2,1)}, bf16[2,128,1536]{2,1,0:T(8,128)(2,1)}, u32[]{:S(2)}, u32[]{:S(2)}) collective-permute-start(bf16[2,128,1536]{2,1,0:T(8,128)(2,1)} %param.10), channel_id=1, source_target_pairs={{96,0},{128,32},{160,64},{192,96},{224,128},{256,160},{288,192},{3... | collective-permute-start | bytes 2359304 | tf_op jit(solution)/shard_map/ppermute | solution.py:14
  25.5 1.3 copy-start.2
  25.5 67.6 %collective-permute-start.4 = (bf16[2,128,1536]{2,1,0:T(8,128)(2,1)}, bf16[2,128,1536]{2,1,0:T(8,128)(2,1)}, u32[]{:S(2)}, u32[]{:S(2)}) collective-permute-start(bf16[2,128,1536]{2,1,0:T(8,128)(2,1)} %param.10), channel_id=1, source_target_pairs={{64,0},{96,32},{128,64},{160,96},{192,128},{224,160},{256,192},{28... | collective-permute-start | bytes 2359304 | tf_op jit(solution)/shard_map/ppermute | solution.py:14
  301.1 86.3 %all-to-all-start = ((bf16[32,128,192]{1,2,0:T(8,128)(2,1)}), bf16[32,128,192]{1,2,0:T(8,128)(2,1)}, u32[]{:S(2)}, u32[]{:S(2)}) async-start(bf16[32,128,192]{1,2,0:T(8,128)(2,1)} %bitcast.54), calls=%async_computation | async-start | bytes 3145728 | tf_op jit(solution)/shard_map/all_to_all | solution.py:79
  391.9 2.4 copy-start.3
  506.5 1.9 copy-start.1
Sparse Core Ops, SparseCore 0:
  12.1 249.1 all-gather.2
where the time goes:
time: 517 us; the launch traced here: 515 us
  waiting for transfers between devices  290 us (56%)
  local copies, waits for them, and re-layouts  72.4 us (14%)
  other arithmetic  39.6 us (8%)
  blocking collectives  36.7 us (7%)
  matrix products  35.9 us (7%)
  starting transfers between devices  26.4 us (5%)
  between operations  14.4 us (3%)
    all_gather x1, waiting for transfers between devices, local(): lax.all_gather(qkv_weight, ('particle', 'seq'), axis=0, tiled=True)  161 us
    all_to_all x1, waiting for transfers between devices, local(): lax.all_to_all(qkv, 'seq', split_axis=0, concat_axis=1, tiled=True)  77.7 us
    ppermute x6, waiting for transfers between devices, shifted(): lax.ppermute(value, axis, [(source, source + steps) for source in range(i...  50.3 us
    all_to_all x1, blocking collectives, local(): lax.all_to_all(attended, 'seq', split_axis=1, concat_axis=0, tiled=True)  36.7 us
    unnamed x14, local copies, waits for them, and re-layouts  28.3 us
    unnamed x1, other arithmetic  23.4 us
    ppermute x6, starting transfers between devices, shifted(): lax.ppermute(value, axis, [(source, source + steps) for source in range(i...  18.1 us
    dot_general x8, matrix products, block_attend(): jnp.dot(query, keys.T, preferred_element_type=jnp.float32) * HD ** (-0.5)  17.7 us
  transfers between devices with their start and end apart: 8, of which 5 were waited for; matrix products, arithmetic and copies ran while one was open for 5% of the time, Pallas kernels for 0%

commit v1 on v0

v1 whole, which is shorter than its diff:
```python
import functools

import jax
import jax.numpy as jnp
from jax import lax
from jax.experimental import pallas as pl
from jax.experimental.pallas import tpu as pltpu
from jax.sharding import PartitionSpec as P

HEADS = 16
HD = 64
PER_PROMPT = 8
MESH = pl.DeviceIdType.MESH
KEYS = 256
LOG2E = 1.4426950408889634


def low_lanes(shape):
    return lax.broadcasted_iota(jnp.int32, shape, len(shape) - 1) < HD


def swap_halves(value):
    return pltpu.roll(value, HD, len(value.shape) - 1)


def send(src, dst, send_sem, recv_sem, column, seq):
    return pltpu.make_async_remote_copy(
        src_ref=src, dst_ref=dst, send_sem=send_sem, recv_sem=recv_sem,
        device_id=(column, seq), device_id_type=MESH,
    )


def block_kernel(
    cols, ring, columns, seqs, txt,
    anc_ref, lat_ref, mod_ref, weight_ref, text_ref, out_ref,
    mod_all, wbuf, kv_out, q_out, kv_all, q_all, scores, o_out, o_all, chosen,
    x_send, x_recv, w_send, w_recv, kv_send, kv_recv, q_send, q_recv, o_send, o_recv, f_send, f_recv,
):
    part_dev, rows, width = lat_ref.shape
    particles = ring * part_dev
    half = rows // 2
    column, me = lax.axis_index("particle"), lax.axis_index("seq")
    first, x = column // ring * ring, column % ring
    left, right = first + (x + ring - 1) % ring, first + (x + 1) % ring
    wrows = weight_ref.shape[1]

    barrier = pltpu.get_barrier_semaphore()

    def greet_seq(k, _):
        pl.semaphore_signal(barrier, inc=1, device_id=(column, (me + k) % seqs), device_id_type=MESH)
        return 0

    def greet_column(k, _):
        pl.semaphore_signal(barrier, inc=1, device_id=((column + k) % columns, me), device_id_type=MESH)
        return 0

    lax.fori_loop(1, seqs, greet_seq, 0)
    lax.fori_loop(1, columns, greet_column, 0)
    pl.semaphore_wait(barrier, seqs + columns - 2)

    def weight_copy(k):
        other = (column + k) % columns
        return send(
            weight_ref.at[other % ring], wbuf.at[pl.ds(pl.multiple_of(column * wrows, wrows), wrows)],
            w_send.at[k], w_recv.at[column], other, me,
        )

    def weight_start(k, _):
        weight_copy(k).start()
        return 0

    lax.fori_loop(1, columns, weight_start, 0)
    own_weight = pltpu.make_async_copy(
        weight_ref.at[x], wbuf.at[pl.ds(pl.multiple_of(column * wrows, wrows), wrows)], w_send.at[0])
    own_weight.start()

    def slot(offset, part):
        return ((x + offset + ring) % ring) * part_dev + part

    def ring_copy(offset, part, leg, target):
        ref = mod_all.at[slot(offset, part)]
        return send(ref, ref, x_send.at[leg, part], x_recv.at[leg, part], target, me)

    shift, scale = mod_ref[0:1, 0:width], mod_ref[0:1, width:2 * width]
    for part in range(part_dev):
        values = lat_ref[part].astype(jnp.float32)
        mean = jnp.mean(values, axis=-1, keepdims=True)
        centred = values - mean
        var = jnp.mean(centred * centred, axis=-1, keepdims=True)
        normed = centred / jnp.sqrt(var + 1e-06)
        mod_all[slot(0, part)] = (normed * (1.0 + scale) + shift).astype(jnp.bfloat16)
        ring_copy(0, part, 0, right).start()
        ring_copy(0, part, 1, left).start()

    def item_seq(part, head):
        return head * particles + part

    def kv_copy(part, head):
        return send(
            kv_out.at[part, head], kv_all.at[pl.ds(pl.multiple_of(me * rows, rows), rows)],
            kv_send.at[item_seq(part, head)], kv_recv.at[me], column, item_seq(part, head),
        )

    def q_copy(part, head):
        return send(
            q_out.at[part, head], q_all.at[me],
            q_send.at[item_seq(part, head)], q_recv.at[me], column, item_seq(part, head),
        )

    def post(copy, own, part, head):
        target = item_seq(part, head)

        @pl.when(target != me)
        def _():
            copy(part, head).start()

        @pl.when(target == me)
        def _():
            own(part, head).start()

    def kv_own(part, head):
        return pltpu.make_async_copy(
            kv_out.at[part, head], kv_all.at[pl.ds(pl.multiple_of(me * rows, rows), rows)], kv_recv.at[me])

    def q_own(part, head):
        return pltpu.make_async_copy(q_out.at[part, head], q_all.at[me], q_recv.at[me])

    def project(offset):
        base = slot(offset, 0)
        states = mod_all[pl.ds(base, part_dev)].reshape(part_dev * rows, width)
        for group in range(cols // 2):
            lanes = slice((cols // 2) * 128 + group * 256, (cols // 2) * 128 + (group + 1) * 256)
            kv = jnp.dot(states, wbuf[:, lanes], preferred_element_type=jnp.float32)
            for part in range(part_dev):
                for side in range(2):
                    piece = kv[part * rows:(part + 1) * rows, side * 128:(side + 1) * 128]
                    kv_out[base + part, 2 * group + side] = piece.astype(jnp.bfloat16)
                    post(kv_copy, kv_own, base + part, 2 * group + side)
        query = jnp.dot(states, wbuf[:, 0:(cols // 2) * 128], preferred_element_type=jnp.float32)
        low = low_lanes((half, 128))
        for part in range(part_dev):
            for group in range(cols // 2):
                lanes = slice(group * 128, (group + 1) * 128)
                upper = query[part * rows:part * rows + half, lanes]
                lower = query[part * rows + half:(part + 1) * rows, lanes]
                q_out[base + part, 2 * group] = jnp.where(low, upper, swap_halves(lower)).astype(jnp.bfloat16)
                q_out[base + part, 2 * group + 1] = jnp.where(low, swap_halves(upper), lower).astype(jnp.bfloat16)

    own_weight.wait()

    def weight_wait(k, _):
        copy = send(
            weight_ref.at[0], wbuf.at[pl.ds(pl.multiple_of(((column + k) % columns) * wrows, wrows), wrows)],
            w_send.at[k], w_recv.at[(column + k) % columns], column, me)
        copy.wait_recv()
        return 0

    lax.fori_loop(1, columns, weight_wait, 0)
    project(0)
    for part in range(part_dev):
        ring_copy(-1, part, 0, right).wait_recv()
        ring_copy(1, part, 1, left).wait_recv()
    ring_copy(-1, 0, 2, right).start()
    ring_copy(1, 1, 2, left).start()
    project(-1)
    project(1)
    for part in range(part_dev):
        ring_copy(2, part, 2, right).wait_recv()
    project(2)
    for offset in (0, -1, 1, 2):
        for part in range(part_dev):
            for head in range(cols):
                post(q_copy, q_own, slot(offset, part), head)

    image = seqs * rows
    kv_all[image:image + KEYS] = text_ref[...]

    def kv_wait(k, _):
        src = (me + k) % seqs
        send(
            kv_out.at[0, 0], kv_all.at[pl.ds(pl.multiple_of(src * rows, rows), rows)],
            kv_send.at[0], kv_recv.at[src], column, me).wait_recv()
        return 0

    lax.fori_loop(0, seqs, kv_wait, 0)

    block = 2 * rows
    chunks = image // KEYS + 1
    factor = HD ** (-0.5) * LOG2E

    def o_copy(src, target):
        return send(o_out.at[src], o_all.at[me], o_send.at[src], o_recv.at[me], column, target)

    def attend(step, _):
        pair = (me // 2 + step) % (seqs // 2)
        queries = []
        low = low_lanes((half, 128))
        for side in range(2):
            src = 2 * pair + side
            send(q_out.at[0, 0], q_all.at[src], q_send.at[0], q_recv.at[src], column, me).wait_recv()
            packed = q_all[src].astype(jnp.float32)
            queries.append(jnp.where(low, packed, 0.0).astype(jnp.bfloat16))
            queries.append(jnp.where(low, swap_halves(packed), 0.0).astype(jnp.bfloat16))
        query = jnp.concatenate(queries, axis=0)
        top = jnp.full((block, 128), -jnp.inf, jnp.float32)
        for chunk in range(chunks):
            keys = kv_all[chunk * KEYS:(chunk + 1) * KEYS]
            part_scores = lax.dot_general(
                query, keys, (((1,), (1,)), ((), ())), preferred_element_type=jnp.float32)
            if chunk == chunks - 1:
                lane = lax.broadcasted_iota(jnp.int32, part_scores.shape, 1)
                part_scores = jnp.where(lane < txt, part_scores, -jnp.inf)
            scores[:, chunk * KEYS:(chunk + 1) * KEYS] = part_scores
            for piece in range(KEYS // 128):
                top = jnp.maximum(top, part_scores[:, piece * 128:(piece + 1) * 128])
        top = jnp.max(top, axis=1, keepdims=True)
        total = jnp.zeros((block, 128), jnp.float32)
        mixed = jnp.zeros((block, 128), jnp.float32)
        for chunk in range(chunks):
            expo = jnp.exp2((scores[:, chunk * KEYS:(chunk + 1) * KEYS] - top) * factor)
            for piece in range(KEYS // 128):
                total = total + expo[:, piece * 128:(piece + 1) * 128]
            mixed = mixed + jnp.dot(
                expo.astype(jnp.bfloat16), kv_all[chunk * KEYS:(chunk + 1) * KEYS],
                preferred_element_type=jnp.float32)
        result = mixed / jnp.sum(total, axis=1, keepdims=True)
        for side in range(2):
            target = 2 * pair + side
            upper = result[side * rows:side * rows + half]
            lower = result[side * rows + half:(side + 1) * rows]
            o_out[target] = jnp.where(low, swap_halves(upper), lower).astype(jnp.bfloat16)

            @pl.when(target != me)
            def _():
                o_copy(target, target).start()

            @pl.when(target == me)
            def _():
                pltpu.make_async_copy(o_out.at[target], o_all.at[me], o_recv.at[me]).start()
        return 0

    lax.fori_loop(0, seqs // 2, attend, 0)

    def o_wait(k, _):
        src = (me + k) % seqs
        send(o_out.at[0], o_all.at[src], o_send.at[0], o_recv.at[src], column, me).wait_recv()
        return 0

    lax.fori_loop(0, seqs, o_wait, 0)
    low = low_lanes((half, 128))

    def final_copy(k):
        lanes = pl.ds(pl.multiple_of(x * (cols * HD), 128), cols * HD)
        return send(
            chosen.at[k], out_ref.at[:, :, lanes], f_send.at[k], f_recv.at[(ring - k) % ring],
            first + (x + k) % ring, me)

    for k in (2, 1, 3, 0):
        goal = (x + k) % ring
        for part in range(part_dev):
            source = anc_ref[(first + goal) * part_dev + part] % particles
            for group in range(cols // 2):
                even = o_all[2 * group * particles + source].astype(jnp.float32)
                odd = o_all[(2 * group + 1) * particles + source].astype(jnp.float32)
                lanes = slice(group * 128, (group + 1) * 128)
                chosen[k, part, 0:half, lanes] = jnp.where(low, even, swap_halves(odd)).astype(jnp.bfloat16)
                chosen[k, part, half:rows, lanes] = jnp.where(low, swap_halves(even), odd).astype(jnp.bfloat16)
        if k:
            final_copy(k).start()
    own_final = pltpu.make_async_copy(
        chosen.at[0], out_ref.at[:, :, pl.ds(pl.multiple_of(x * (cols * HD), 128), cols * HD)], f_send.at[0])
    own_final.start()
    own_final.wait()

    for part in range(part_dev):
        ring_copy(0, part, 0, right).wait_send()
        ring_copy(0, part, 1, left).wait_send()
    ring_copy(-1, 0, 2, right).wait_send()
    ring_copy(1, 1, 2, left).wait_send()

    def weight_sent(k, _):
        weight_copy(k).wait_send()
        return 0

    lax.fori_loop(1, columns, weight_sent, 0)

    def item_sent(k, _):
        target = (me + k) % seqs
        part, head = target % particles, target // particles
        kv_copy(part, head).wait_send()
        q_copy(part, head).wait_send()
        o_copy(target, target).wait_send()
        return 0

    lax.fori_loop(1, seqs, item_sent, 0)
    for k in range(1, ring):
        final_copy(k).wait_send()
        lanes = pl.ds(pl.multiple_of((x + k) % ring * (cols * HD), 128), cols * HD)
        send(
            chosen.at[k], out_ref.at[:, :, lanes], f_send.at[k], f_recv.at[k],
            column, me).wait_recv()


def local(columns, seqs, latents, mod_table, step_index, qkv_weight, text_kv, ancestors):
    part_dev, rows, width = latents.shape
    ring = PER_PROMPT // part_dev
    cols = HEADS // ring
    txt = text_kv.shape[1]
    column, me = lax.axis_index("particle"), lax.axis_index("seq")
    modrow = lax.dynamic_slice_in_dim(mod_table, step_index[0], 1, 0)
    wrows = qkv_weight.shape[0]
    by_head = qkv_weight.reshape(wrows, ring, cols, 3 * HD)
    arranged = jnp.concatenate([
        by_head[..., 0:HD].reshape(wrows, ring, cols * HD),
        by_head[..., HD:3 * HD].reshape(wrows, ring, 2 * cols * HD),
    ], axis=2).reshape(wrows, ring * 3 * cols * HD)
    weight = lax.all_gather(arranged, "seq", axis=0, tiled=True)
    weight = weight.reshape(seqs * wrows, ring, 3 * cols * HD).transpose(1, 0, 2)
    text_row = column // ring * HEADS + column % ring * cols + me // PER_PROMPT
    text = lax.dynamic_index_in_dim(text_kv, text_row, 0, keepdims=False)
    text = jnp.pad(text, ((0, KEYS - txt), (0, 0)))
    items = PER_PROMPT * cols
    chunks = seqs * rows // KEYS + 1
    bf16, f32 = jnp.bfloat16, jnp.float32
    vmem, dma = pltpu.VMEM, pltpu.SemaphoreType.DMA
    return pl.pallas_call(
        functools.partial(block_kernel, cols, ring, columns, seqs, txt),
        out_shape=jax.ShapeDtypeStruct((part_dev, rows, HEADS * HD), bf16),
        in_specs=[pl.BlockSpec(memory_space=pltpu.SMEM)] + [pl.BlockSpec(memory_space=pltpu.VMEM)] * 4,
        out_specs=pl.BlockSpec(memory_space=pltpu.VMEM),
        scratch_shapes=[
            vmem((PER_PROMPT, rows, width), bf16),
            vmem((columns * seqs * wrows, 3 * cols * HD), bf16),
            vmem((PER_PROMPT, cols, rows, 128), bf16),
            vmem((PER_PROMPT, cols, rows // 2, 128), bf16),
            vmem((seqs * rows + KEYS, 128), bf16),
            vmem((seqs, rows // 2, 128), bf16),
            vmem((2 * rows, chunks * KEYS), f32),
            vmem((seqs, rows // 2, 128), bf16),
            vmem((seqs, rows // 2, 128), bf16),
            vmem((ring, part_dev, rows, cols * HD), bf16),
            dma((3, part_dev)), dma((3, part_dev)),
            dma((columns,)), dma((columns,)),
            dma((items,)), dma((items,)), dma((items,)), dma((items,)), dma((items,)), dma((items,)),
            dma((ring,)), dma((ring,)),
        ],
        compiler_params=pltpu.CompilerParams(
            collective_id=0, has_side_effects=True, vmem_limit_bytes=48 * 2**20),
        cost_estimate=pl.CostEstimate(flops=7 * 10**9, bytes_accessed=4 * 10**6, transcendentals=18 * 10**6),
        name="steered_block",
    )(ancestors, latents, modrow, weight, text)


def solution(mesh):
    in_specs = (P("particle", "seq", None), P(), P(), P(("particle", "seq"), None), P(), P())
    out_specs = P("particle", "seq", None)
    body = functools.partial(local, mesh.shape["particle"], mesh.shape["seq"])
    return jax.shard_map(body, mesh=mesh, in_specs=in_specs, out_specs=out_specs, check_vma=False)
```

time: 517 us -> 222 us (0.43)
  waiting for transfers between devices: 290 us -> 0 us
  Pallas kernels: 0 us -> 171 us
  local copies, waits for them, and re-layouts: 72.4 us -> 7.34 us
  other arithmetic: 39.6 us -> 0.01 us
  matrix products: 35.9 us -> 0 us
  starting transfers between devices: 26.4 us -> 0 us
  between operations: 14.4 us -> 0.93 us
  blocking collectives: 36.7 us -> 42.4 us
    pallas_call x0 -> x1, Pallas kernels: none -> 171 us  [local(): pl.pallas_call(functools.partial(block_kernel, cols, ring, columns, seqs,...]
    all_gather x1 -> x0, waiting for transfers between devices: 161 us -> none  [local(): lax.all_gather(qkv_weight, ('particle', 'seq'), axis=0, tiled=True)]
    all_to_all x1 -> x0, waiting for transfers between devices: 77.7 us -> none  [local(): lax.all_to_all(qkv, 'seq', split_axis=0, concat_axis=1, tiled=True)]
    ppermute x6 -> x0, waiting for transfers between devices: 50.3 us -> none  [shifted(): lax.ppermute(value, axis, [(source, source + steps) for source in range(i...]
    all_gather x0 -> x1, blocking collectives: none -> 42.4 us  [local(): weight = lax.all_gather(arranged, 'seq', axis=0, tiled=True)]
    all_to_all x1 -> x0, blocking collectives: 36.7 us -> none  [local(): lax.all_to_all(attended, 'seq', split_axis=1, concat_axis=0, tiled=True)]
    dot_general x17 -> x0, matrix products: 35.9 us -> none  [the longest x8 17.7 us: block_attend(): jnp.dot(query, keys.T, preferred_element_type=jnp.float32) * HD ** (-0.5)]
    unnamed x14 -> x9, local copies, waits for them, and re-layouts: 28.3 us -> 1.96 us
  transfers between devices with their start and end apart: 8 -> 0, of which waited for: 5 -> 0; matrix products, arithmetic and copies ran while one was open for 5% -> 0% of each run, Pallas kernels for 0% -> 0%
where the time goes in v1:
time: 222 us; the launch traced here: 221 us
  Pallas kernels  171 us (77%)
  blocking collectives  42.4 us (19%)
  local copies, waits for them, and re-layouts  7.34 us (3%)
    pallas_call x1, Pallas kernels, local(): pl.pallas_call(functools.partial(block_kernel, cols, ring, columns, seqs,...  171 us
    all_gather x1, blocking collectives, local(): weight = lax.all_gather(arranged, 'seq', axis=0, tiled=True)  42.4 us

profile of v1, /device:TPU:1, one launch (start us, length us, event | category | flops | bytes accessed | tf_op | source)
XLA Modules:
  0.0 221.3 jit_solution(9412982185718164023)
XLA Ops:
  0.0 0.0 copy-start
  0.0 0.0 copy-start.2
  0.8 0.9 constant_dynamic-slice_fusion.1.mod_ref
  1.7 0.8 reshape.15
  2.6 0.1 slice.9
  2.7 0.1 reshape.16
  2.8 42.4 %all-gather = bf16[32,3,3072]{2,1,0:T(4,128)(2,1)} all-gather(bf16[1,3,3072]{2,1,0:T(4,128)(2,1)S(1)} %reshape.20), channel_id=1, replica_groups=mesh['particle'=16,'seq'=32] {'seq'}, dimensions={0}, use_global_device_ids=true | all-gather | bytes 608256 | tf_op jit(solution)/shard_map/all_gather | solution.py:317
  45.2 2.2 %reshape.19 = bf16[96,4,768]{2,1,0:T(4,128)(2,1)} reshape(bf16[32,3,3072]{2,1,0:T(4,128)(2,1)} %all-gather) | data formatting | bytes 1179648 | tf_op jit(solution)/shard_map/reshape | solution.py:318
  47.4 1.1 copy.14
  48.6 0.0 copy-done
  48.6 0.1 constant_dynamic-slice_fusion
  48.7 0.0 copy-done.2
  48.7 0.0 copy-start.1
  48.7 1.1 copy-done.1
  49.9 170.7 %steered_block.1 = bf16[2,128,1024]{2,1,0:T(8,128)(2,1)S(1)} custom-call(s32[32]{0:T(128)S(1)} %copy-done.2, bf16[2,128,1536]{2,1,0:T(8,128)(2,1)S(1)} %copy-done.1, f32[1,3072]{1,0:T(1,128)S(1)} %constant_dynamic-slice_fusion.1.mod_ref, bf16[4,96,768]{2,1,0:T(8,128)(2,1)S(1)} %bitcast.10, bf16[256,128]{1,0:T(8,128)(2,1)S(1)} %pad.4.text_ref), custom_call_target="tpu_custom_call" | custom-call | flops 7000000000 | bytes 4000000 | tf_op jit(solution)/shard_map/steered_block/pallas_call | solution.py:326
  220.5 0.8 copy.18
  (6 shorter events, 0.1 us)
Async XLA Ops:
  0.0 48.6 %copy-start = (bf16[64,154,128]{2,0,1:T(8,128)(2,1)S(1)}, bf16[64,154,128]{2,0,1:T(8,128)(2,1)}, u32[]{:S(2)}) copy-start(bf16[64,154,128]{2,0,1:T(8,128)(2,1)} %param.10) | copy-start | bytes 7569412
  0.0 48.7 %copy-start.2 = (s32[32]{0:T(128)S(1)}, s32[32]{0:T(128)}, u32[]{:S(2)}) copy-start(s32[32]{0:T(128)} %anc_ref.1) | copy-start | bytes 388
  48.7 1.1 copy-start.1

commit v2 on v1

--- a/solution.py
+++ b/solution.py
@@ -12,6 +12,10 @@
 PER_PROMPT = 8
 MESH = pl.DeviceIdType.MESH
 KEYS = 256
+FORWARD_AT = 4
+TEXT_PAD = 160
+SLICES = 4
+ROW_PAD = 8
 LOG2E = 1.4426950408889634
 
 
@@ -30,11 +34,28 @@
     )
 
 
+def pack_weight(weight_ref, wsend, ring, cols):
+    shard = weight_ref[...].astype(jnp.float32)
+    count = shard.shape[0]
+    for r in range(ring):
+        for group in range(3 * cols // 2):
+            if group < cols // 2:
+                start = (r * cols + 2 * group) * 3 * HD
+                piece = jnp.concatenate([shard[:, start:start + HD], shard[:, start + 3 * HD:start + 4 * HD]], axis=1)
+            else:
+                start = (r * cols + group - cols // 2) * 3 * HD + HD
+                piece = shard[:, start:start + 2 * HD]
+            for i in range(count):
+                wsend[r, i, group:group + 1, :] = piece[i:i + 1]
+
+
 def block_kernel(
     cols, ring, columns, seqs, txt,
-    anc_ref, lat_ref, mod_ref, weight_ref, text_ref, out_ref,
-    mod_all, wbuf, kv_out, q_out, kv_all, q_all, scores, o_out, o_all, chosen,
-    x_send, x_recv, w_send, w_recv, kv_send, kv_recv, q_send, q_recv, o_send, o_recv, f_send, f_recv,
+    anc_ref, step_ref, lat_ref, mod_ref, weight_ref, text_hbm, out_ref,
+    mod_all, order, wsend, wplane, wbuf, kv_out, q_out, kv_all, values_t, q_all, text_buf,
+    scores, probs, o_out, o_all, chosen,
+    x_send, x_recv, p_send, p_recv, w_send, w_recv, t_sem,
+    kv_send, kv_recv, q_send, q_recv, o_send, o_recv, f_send, f_recv,
 ):
     part_dev, rows, width = lat_ref.shape
     particles = ring * part_dev
@@ -42,7 +63,8 @@
     column, me = lax.axis_index("particle"), lax.axis_index("seq")
     first, x = column // ring * ring, column % ring
     left, right = first + (x + ring - 1) % ring, first + (x + 1) % ring
-    wrows = weight_ref.shape[1]
+    wrows = weight_ref.shape[0]
+    image = seqs * rows
 
     barrier = pltpu.get_barrier_semaphore()
 
@@ -56,23 +78,31 @@
 
     lax.fori_loop(1, seqs, greet_seq, 0)
     lax.fori_loop(1, columns, greet_column, 0)
+
+    text_row = column // ring * HEADS + x * cols + me // particles
+    text_copy = pltpu.make_async_copy(text_hbm.at[text_row], text_buf, t_sem)
+    text_copy.start()
+    pack_weight(weight_ref, wsend, ring, cols)
+    span = seqs * wrows
+    local_row = lax.broadcasted_iota(jnp.int32, (span, 1), 0)
+    owner = lax.shift_right_logical(local_row * 43691, 17)
+    place = owner * (wrows * columns) + (local_row - owner * wrows) * columns
+    lane = lax.broadcasted_iota(jnp.int32, (span, width), 1)
+    for c in range(columns):
+        order[c * span:(c + 1) * span] = jnp.where(lane == place + c, 1.0, 0.0).astype(jnp.bfloat16)
     pl.semaphore_wait(barrier, seqs + columns - 2)
 
-    def weight_copy(k):
+    def plane_copy(k):
         other = (column + k) % columns
-        return send(
-            weight_ref.at[other % ring], wbuf.at[pl.ds(pl.multiple_of(column * wrows, wrows), wrows)],
-            w_send.at[k], w_recv.at[column], other, me,
-        )
-
-    def weight_start(k, _):
-        weight_copy(k).start()
-        return 0
-
-    lax.fori_loop(1, columns, weight_start, 0)
-    own_weight = pltpu.make_async_copy(
-        weight_ref.at[x], wbuf.at[pl.ds(pl.multiple_of(column * wrows, wrows), wrows)], w_send.at[0])
-    own_weight.start()
+        return send(wsend.at[other % ring], wplane.at[column], p_send.at[k], p_recv.at[column], other, me)
+
+    def plane_start(k, _):
+        plane_copy(k).start()
+        return 0
+
+    lax.fori_loop(1, columns, plane_start, 0)
+    plane_own = pltpu.make_async_copy(wsend.at[x], wplane.at[column], p_recv.at[column])
+    plane_own.start()
 
     def slot(offset, part):
         return ((x + offset + ring) % ring) * part_dev + part
@@ -81,16 +111,19 @@
         ref = mod_all.at[slot(offset, part)]
         return send(ref, ref, x_send.at[leg, part], x_recv.at[leg, part], target, me)
 
-    shift, scale = mod_ref[0:1, 0:width], mod_ref[0:1, width:2 * width]
+    mod_row = mod_ref[pl.ds(step_ref[0], 1), :]
+    shift, scale = mod_row[:, 0:width], mod_row[:, width:2 * width]
     for part in range(part_dev):
         values = lat_ref[part].astype(jnp.float32)
         mean = jnp.mean(values, axis=-1, keepdims=True)
         centred = values - mean
         var = jnp.mean(centred * centred, axis=-1, keepdims=True)
         normed = centred / jnp.sqrt(var + 1e-06)
-        mod_all[slot(0, part)] = (normed * (1.0 + scale) + shift).astype(jnp.bfloat16)
+        modded = (normed * (1.0 + scale) + shift).astype(jnp.bfloat16)
+        mod_all[slot(0, part)] = jnp.dot(modded, order[...], preferred_element_type=jnp.float32).astype(jnp.bfloat16)
+    for part in range(part_dev):
         ring_copy(0, part, 0, right).start()
-        ring_copy(0, part, 1, left).start()
+        ring_copy(0, part_dev - 1 - part, 1, left).start()
 
     def item_seq(part, head):
         return head * particles + part
@@ -146,22 +179,71 @@
                 q_out[base + part, 2 * group] = jnp.where(low, upper, swap_halves(lower)).astype(jnp.bfloat16)
                 q_out[base + part, 2 * group + 1] = jnp.where(low, swap_halves(upper), lower).astype(jnp.bfloat16)
 
-    own_weight.wait()
-
-    def weight_wait(k, _):
-        copy = send(
-            weight_ref.at[0], wbuf.at[pl.ds(pl.multiple_of(((column + k) % columns) * wrows, wrows), wrows)],
-            w_send.at[k], w_recv.at[(column + k) % columns], column, me)
-        copy.wait_recv()
-        return 0
-
-    lax.fori_loop(1, columns, weight_wait, 0)
+    def plane_wait(k, _):
+        src = (column + k) % columns
+        send(wsend.at[0], wplane.at[src], p_send.at[k], p_recv.at[src], column, me).wait_recv()
+        return 0
+
+    lax.fori_loop(0, columns, plane_wait, 0)
+    block_rows = wrows * columns
+
+    def weight_rows(index):
+        return wbuf.at[pl.ds(pl.multiple_of(index * block_rows, block_rows), block_rows)]
+
+    base_row = pl.multiple_of(me * block_rows, block_rows)
+    for group in range(3 * cols // 2):
+        for i in range(wrows):
+            wbuf[pl.ds(base_row + i * columns, columns), group * 128:(group + 1) * 128] = (
+                wplane[:, i, group, :].astype(jnp.bfloat16))
+    chips = seqs // 2
+    sibling = me + 1 - 2 * (me % 2)
+
+    def around(hops):
+        return (me + 2 * hops + seqs) % seqs
+
+    def weight_copy(index, leg, hop, target):
+        return send(weight_rows(index), weight_rows(index), w_send.at[leg, hop], w_recv.at[index], column, target)
+
+    def weight_wait(index):
+        weight_copy(index, 0, 0, me).wait_recv()
+
+    reach = (chips // 2, chips - 1 - chips // 2)
+    started = []
+
+    def weight_start(*args):
+        copy = weight_copy(*args)
+        copy.start()
+        started.append(copy)
+
+    weight_start(me, 0, 0, around(1))
+    weight_start(me, 1, 0, around(-1))
+    weight_start(me, 2, 0, sibling)
+    for hop in range(1, reach[0] + 1):
+        index = around(-hop)
+        weight_wait(index)
+        if hop < reach[0]:
+            weight_start(index, 0, hop, around(1))
+        weight_start(index, 2, hop, sibling)
+        if hop <= reach[1]:
+            index = around(hop)
+            weight_wait(index)
+            if hop < reach[1]:
+                weight_start(index, 1, hop, around(-1))
+            weight_start(index, 3, hop, sibling)
+        if hop == FORWARD_AT:
+            ring_copy(-1, 0, 0, right).wait_recv()
+            ring_copy(-1, 0, 2, right).start()
+            ring_copy(1, 1, 1, left).wait_recv()
+            ring_copy(1, 1, 2, left).start()
+
+    def sibling_wait(k, _):
+        weight_wait((sibling + 2 * k) % seqs)
+        return 0
+
+    lax.fori_loop(0, chips, sibling_wait, 0)
     project(0)
-    for part in range(part_dev):
-        ring_copy(-1, part, 0, right).wait_recv()
-        ring_copy(1, part, 1, left).wait_recv()
-    ring_copy(-1, 0, 2, right).start()
-    ring_copy(1, 1, 2, left).start()
+    ring_copy(-1, 1, 0, right).wait_recv()
+    ring_copy(1, 0, 1, left).wait_recv()
     project(-1)
     project(1)
     for part in range(part_dev):
@@ -172,8 +254,9 @@
             for head in range(cols):
                 post(q_copy, q_own, slot(offset, part), head)
 
-    image = seqs * rows
-    kv_all[image:image + KEYS] = text_ref[...]
+    text_copy.wait()
+    kv_all[image:image + TEXT_PAD] = jnp.zeros((TEXT_PAD, 128), jnp.bfloat16)
+    kv_all[image:image + txt] = text_buf[...]
 
     def kv_wait(k, _):
         src = (me + k) % seqs
@@ -184,51 +267,57 @@
 
     lax.fori_loop(0, seqs, kv_wait, 0)
 
-    block = 2 * rows
-    chunks = image // KEYS + 1
+    joint = image + TEXT_PAD
+    bounds = [(low, min(KEYS, joint - low)) for low in range(0, joint, KEYS)]
+    for low, count in bounds:
+        turned = kv_all[low:low + count].astype(jnp.float32).T
+        values_t[:, low:low + count] = turned[HD:2 * HD].astype(jnp.bfloat16)
+
+    block = SLICES * rows
     factor = HD ** (-0.5) * LOG2E
 
     def o_copy(src, target):
         return send(o_out.at[src], o_all.at[me], o_send.at[src], o_recv.at[me], column, target)
 
+    def fold(value, op):
+        result = value[0:8]
+        for row in range(8, value.shape[0], 8):
+            result = op(result, value[row:row + 8])
+        return result
+
     def attend(step, _):
-        pair = (me // 2 + step) % (seqs // 2)
+        base = (me // SLICES + step) % (seqs // SLICES) * SLICES
         queries = []
-        low = low_lanes((half, 128))
-        for side in range(2):
-            src = 2 * pair + side
+        lower_lanes = low_lanes((half, 128))
+        for side in range(SLICES):
+            src = base + side
             send(q_out.at[0, 0], q_all.at[src], q_send.at[0], q_recv.at[src], column, me).wait_recv()
             packed = q_all[src].astype(jnp.float32)
-            queries.append(jnp.where(low, packed, 0.0).astype(jnp.bfloat16))
-            queries.append(jnp.where(low, swap_halves(packed), 0.0).astype(jnp.bfloat16))
+            queries.append(jnp.where(lower_lanes, packed, 0.0).astype(jnp.bfloat16))
+            queries.append(jnp.where(lower_lanes, swap_halves(packed), 0.0).astype(jnp.bfloat16))
         query = jnp.concatenate(queries, axis=0)
-        top = jnp.full((block, 128), -jnp.inf, jnp.float32)
-        for chunk in range(chunks):
-            keys = kv_all[chunk * KEYS:(chunk + 1) * KEYS]
+        top = jnp.full((8, block), -jnp.inf, jnp.float32)
+        for low, count in bounds:
             part_scores = lax.dot_general(
-                query, keys, (((1,), (1,)), ((), ())), preferred_element_type=jnp.float32)
-            if chunk == chunks - 1:
-                lane = lax.broadcasted_iota(jnp.int32, part_scores.shape, 1)
-                part_scores = jnp.where(lane < txt, part_scores, -jnp.inf)
-            scores[:, chunk * KEYS:(chunk + 1) * KEYS] = part_scores
-            for piece in range(KEYS // 128):
-                top = jnp.maximum(top, part_scores[:, piece * 128:(piece + 1) * 128])
-        top = jnp.max(top, axis=1, keepdims=True)
-        total = jnp.zeros((block, 128), jnp.float32)
-        mixed = jnp.zeros((block, 128), jnp.float32)
-        for chunk in range(chunks):
-            expo = jnp.exp2((scores[:, chunk * KEYS:(chunk + 1) * KEYS] - top) * factor)
-            for piece in range(KEYS // 128):
-                total = total + expo[:, piece * 128:(piece + 1) * 128]
-            mixed = mixed + jnp.dot(
-                expo.astype(jnp.bfloat16), kv_all[chunk * KEYS:(chunk + 1) * KEYS],
-                preferred_element_type=jnp.float32)
-        result = mixed / jnp.sum(total, axis=1, keepdims=True)
-        for side in range(2):
-            target = 2 * pair + side
+                kv_all[low:low + count], query, (((1,), (1,)), ((), ())), preferred_element_type=jnp.float32)
+            if low + count > image + txt:
+                key = lax.broadcasted_iota(jnp.int32, part_scores.shape, 0) + low
+                part_scores = jnp.where(key < image + txt, part_scores, -jnp.inf)
+            scores[low:low + count] = part_scores
+            top = jnp.maximum(top, fold(part_scores, jnp.maximum))
+        top = jnp.max(top, axis=0, keepdims=True)
+        total = jnp.zeros((8, block), jnp.float32)
+        for low, count in bounds:
+            expo = jnp.exp2((scores[low:low + count] - top) * factor)
+            total = total + fold(expo, jnp.add)
+            probs[low:low + count] = expo.astype(jnp.bfloat16)
+        mixed = jnp.dot(values_t[...], probs[...], preferred_element_type=jnp.float32)
+        result = (mixed / jnp.sum(total, axis=0, keepdims=True)).T
+        for side in range(SLICES):
+            target = base + side
             upper = result[side * rows:side * rows + half]
             lower = result[side * rows + half:(side + 1) * rows]
-            o_out[target] = jnp.where(low, swap_halves(upper), lower).astype(jnp.bfloat16)
+            o_out[target] = jnp.concatenate([upper, lower], axis=1).astype(jnp.bfloat16)
 
             @pl.when(target != me)
             def _():
@@ -239,7 +328,7 @@
                 pltpu.make_async_copy(o_out.at[target], o_all.at[me], o_recv.at[me]).start()
         return 0
 
-    lax.fori_loop(0, seqs // 2, attend, 0)
+    lax.fori_loop(0, seqs // SLICES, attend, 0)
 
     def o_wait(k, _):
         src = (me + k) % seqs
@@ -278,11 +367,13 @@
     ring_copy(-1, 0, 2, right).wait_send()
     ring_copy(1, 1, 2, left).wait_send()
 
-    def weight_sent(k, _):
-        weight_copy(k).wait_send()
-        return 0
-
-    lax.fori_loop(1, columns, weight_sent, 0)
+    def plane_sent(k, _):
+        plane_copy(k).wait_send()
+        return 0
+
+    lax.fori_loop(1, columns, plane_sent, 0)
+    for copy in started:
+        copy.wait_send()
 
     def item_sent(k, _):
         target = (me + k) % seqs
@@ -306,49 +397,45 @@
     ring = PER_PROMPT // part_dev
     cols = HEADS // ring
     txt = text_kv.shape[1]
-    column, me = lax.axis_index("particle"), lax.axis_index("seq")
-    modrow = lax.dynamic_slice_in_dim(mod_table, step_index[0], 1, 0)
     wrows = qkv_weight.shape[0]
-    by_head = qkv_weight.reshape(wrows, ring, cols, 3 * HD)
-    arranged = jnp.concatenate([
-        by_head[..., 0:HD].reshape(wrows, ring, cols * HD),
-        by_head[..., HD:3 * HD].reshape(wrows, ring, 2 * cols * HD),
-    ], axis=2).reshape(wrows, ring * 3 * cols * HD)
-    weight = lax.all_gather(arranged, "seq", axis=0, tiled=True)
-    weight = weight.reshape(seqs * wrows, ring, 3 * cols * HD).transpose(1, 0, 2)
-    text_row = column // ring * HEADS + column % ring * cols + me // PER_PROMPT
-    text = lax.dynamic_index_in_dim(text_kv, text_row, 0, keepdims=False)
-    text = jnp.pad(text, ((0, KEYS - txt), (0, 0)))
     items = PER_PROMPT * cols
-    chunks = seqs * rows // KEYS + 1
+    joint = seqs * rows + TEXT_PAD
     bf16, f32 = jnp.bfloat16, jnp.float32
     vmem, dma = pltpu.VMEM, pltpu.SemaphoreType.DMA
+    smem_spec, vmem_spec = pl.BlockSpec(memory_space=pltpu.SMEM), pl.BlockSpec(memory_space=pltpu.VMEM)
     return pl.pallas_call(
         functools.partial(block_kernel, cols, ring, columns, seqs, txt),
         out_shape=jax.ShapeDtypeStruct((part_dev, rows, HEADS * HD), bf16),
-        in_specs=[pl.BlockSpec(memory_space=pltpu.SMEM)] + [pl.BlockSpec(memory_space=pltpu.VMEM)] * 4,
-        out_specs=pl.BlockSpec(memory_space=pltpu.VMEM),
+        in_specs=[smem_spec, smem_spec, vmem_spec, vmem_spec, vmem_spec, pl.BlockSpec(memory_space=pl.ANY)],
+        out_specs=vmem_spec,
         scratch_shapes=[
             vmem((PER_PROMPT, rows, width), bf16),
-            vmem((columns * seqs * wrows, 3 * cols * HD), bf16),
+            vmem((width, width), bf16),
+            vmem((ring, wrows, ROW_PAD, 128), f32),
+            vmem((columns, wrows, ROW_PAD, 128), f32),
+            vmem((width, 3 * cols * HD), bf16),
             vmem((PER_PROMPT, cols, rows, 128), bf16),
             vmem((PER_PROMPT, cols, rows // 2, 128), bf16),
-            vmem((seqs * rows + KEYS, 128), bf16),
+            vmem((joint, 128), bf16),
+            vmem((HD, joint), bf16),
             vmem((seqs, rows // 2, 128), bf16),
-            vmem((2 * rows, chunks * KEYS), f32),
+            vmem((txt, 128), bf16),
+            vmem((joint, SLICES * rows), f32),
+            vmem((joint, SLICES * rows), bf16),
             vmem((seqs, rows // 2, 128), bf16),
             vmem((seqs, rows // 2, 128), bf16),
             vmem((ring, part_dev, rows, cols * HD), bf16),
             dma((3, part_dev)), dma((3, part_dev)),
             dma((columns,)), dma((columns,)),
+            dma((4, seqs // 4 + 1)), dma((seqs,)), dma,
             dma((items,)), dma((items,)), dma((items,)), dma((items,)), dma((items,)), dma((items,)),
             dma((ring,)), dma((ring,)),
         ],
         compiler_params=pltpu.CompilerParams(
-            collective_id=0, has_side_effects=True, vmem_limit_bytes=48 * 2**20),
+            collective_id=0, has_side_effects=True, vmem_limit_bytes=52 * 2**20),
         cost_estimate=pl.CostEstimate(flops=7 * 10**9, bytes_accessed=4 * 10**6, transcendentals=18 * 10**6),
         name="steered_block",
-    )(ancestors, latents, modrow, weight, text)
+    )(ancestors, step_index, latents, mod_table, qkv_weight, text_kv)
 
 
 def solution(mesh):

time: 222 us -> 173 us (0.78)
  blocking collectives: 42.4 us -> 0 us
  Pallas kernels: 171 us -> 167 us
    all_gather x1 -> x0, blocking collectives: 42.4 us -> none  [local(): weight = lax.all_gather(arranged, 'seq', axis=0, tiled=True)]
    reshape x5 -> x0, local copies, waits for them, and re-layouts: 4.29 us -> none  [the longest x2 3.35 us: local(): weight.reshape(seqs * wrows, ring, 3 * cols * HD).transpose(1, 0, 2)]
    pallas_call x1, Pallas kernels: 171 us -> 167 us  [local(): pl.pallas_call(functools.partial(block_kernel, cols, ring, columns, seqs,...]
    unnamed x9 -> x10, local copies, waits for them, and re-layouts: 1.96 us -> 5.66 us
where the time goes in v2:
time: 173 us
  Pallas kernels  167 us (97%)
  local copies, waits for them, and re-layouts  5.66 us (3%)
    pallas_call x1, Pallas kernels, local(): pl.pallas_call(functools.partial(block_kernel, cols, ring, columns, seqs,...  167 us
    unnamed x10, local copies, waits for them, and re-layouts  5.66 us

profile of v2, /device:TPU:1, one launch (start us, length us, event | category | flops | bytes accessed | tf_op | source)
XLA Modules:
  0.0 173.1 jit_solution(17047956584163382232)
XLA Ops:
  0.0 0.0 copy-start.3
  0.0 0.0 copy-start.2
  0.0 0.0 copy-start.1
  0.0 0.0 copy-start
  0.8 4.8 %copy.7.text_hbm = bf16[64,154,128]{2,1,0:T(8,128)(2,1)} copy(bf16[64,154,128]{2,0,1:T(8,128)(2,1)} %param.10) | data formatting | bytes 5046272 | tf_op args[4]
  5.6 0.0 copy-done.3
  5.6 0.0 copy-done.2
  5.6 0.0 copy-done.1
  5.6 0.0 copy-done
  5.6 166.6 %steered_block.1 = bf16[2,128,1024]{2,1,0:T(8,128)(2,1)S(1)} custom-call(s32[32]{0:T(128)S(1)} %copy-done.3, s32[1]{0:T(128)S(6)} %copy.9.step_ref, bf16[2,128,1536]{2,1,0:T(8,128)(2,1)S(1)} %copy-done, f32[28,3072]{1,0:T(8,128)S(1)} %copy-done.1, bf16[3,3072]{1,0:T(4,128)(2,1)S(1)} %copy-done.2, bf16[64,154,128]{2,1,0:T(8,128)(2,1)} %copy.7.text_hbm), custom_call_target="tpu_custom_call" | custom-call | flops 7000000000 | bytes 4000000 | tf_op jit(solution)/shard_map/steered_block/pallas_call | solution.py:406
  172.3 0.8 copy.10
Async XLA Ops:
  0.0 5.6 %copy-start.3 = (s32[32]{0:T(128)S(1)}, s32[32]{0:T(128)}, u32[]{:S(2)}) copy-start(s32[32]{0:T(128)} %anc_ref.1) | copy-start | bytes 388
  0.0 5.6 %copy-start.2 = (bf16[3,3072]{1,0:T(4,128)(2,1)S(1)}, bf16[3,3072]{1,0:T(4,128)(2,1)}, u32[]{:S(2)}) copy-start(bf16[3,3072]{1,0:T(4,128)(2,1)} %weight_ref.1) | copy-start | bytes 55300
  0.0 5.6 %copy-start.1 = (f32[28,3072]{1,0:T(8,128)S(1)}, f32[28,3072]{1,0:T(8,128)}, u32[]{:S(2)}) copy-start(f32[28,3072]{1,0:T(8,128)} %mod_ref.1) | copy-start | bytes 1032196
  0.0 5.6 %copy-start = (bf16[2,128,1536]{2,1,0:T(8,128)(2,1)S(1)}, bf16[2,128,1536]{2,1,0:T(8,128)(2,1)}, u32[]{:S(2)}) copy-start(bf16[2,128,1536]{2,1,0:T(8,128)(2,1)} %lat_ref.1) | copy-start | bytes 2359300

commit v3 on v2

--- a/solution.py
+++ b/solution.py
@@ -12,9 +12,9 @@
 PER_PROMPT = 8
 MESH = pl.DeviceIdType.MESH
 KEYS = 256
-FORWARD_AT = 4
 TEXT_PAD = 160
 SLICES = 4
+PIECES = 3
 ROW_PAD = 8
 LOG2E = 1.4426950408889634
 
@@ -51,10 +51,10 @@
 
 def block_kernel(
     cols, ring, columns, seqs, txt,
-    anc_ref, step_ref, lat_ref, mod_ref, weight_ref, text_hbm, out_ref,
-    mod_all, order, wsend, wplane, wbuf, kv_out, q_out, kv_all, values_t, q_all, text_buf,
+    step_ref, anc_any, lat_any, mod_any, weight_ref, text_hbm, out_ref,
+    anc_ref, lat_ref, mod_ref, in_sem, mod_all, order, wsend, wplane, wbuf, kv_out, q_out, kv_all, values_t, q_all, text_buf,
     scores, probs, o_out, o_all, chosen,
-    x_send, x_recv, p_send, p_recv, w_send, w_recv, t_sem,
+    x_send, x_recv, p_send, p_recv, z_send, z_recv, y_send, y_recv, b_send, b_recv, t_sem,
     kv_send, kv_recv, q_send, q_recv, o_send, o_recv, f_send, f_recv,
 ):
     part_dev, rows, width = lat_ref.shape
@@ -66,6 +66,13 @@
     wrows = weight_ref.shape[0]
     image = seqs * rows
 
+    inputs = [
+        pltpu.make_async_copy(src, dst, in_sem.at[i])
+        for i, (src, dst) in enumerate(((lat_any, lat_ref), (mod_any, mod_ref), (anc_any, anc_ref)))
+    ]
+    for copy in inputs:
+        copy.start()
+
     barrier = pltpu.get_barrier_semaphore()
 
     def greet_seq(k, _):
@@ -79,30 +86,42 @@
     lax.fori_loop(1, seqs, greet_seq, 0)
     lax.fori_loop(1, columns, greet_column, 0)
 
-    text_row = column // ring * HEADS + x * cols + me // particles
-    text_copy = pltpu.make_async_copy(text_hbm.at[text_row], text_buf, t_sem)
+    text_block = pl.ds(pl.multiple_of(column // ring * HEADS, HEADS), HEADS)
+    text_copy = pltpu.make_async_copy(text_hbm.at[:, text_block, :], text_buf, t_sem)
     text_copy.start()
     pack_weight(weight_ref, wsend, ring, cols)
     span = seqs * wrows
+    chips, planes = seqs // 2, columns // ring
+    per = chips // planes
+    y, z, core = column // ring, me // 2, me % 2
+
+    def arrival(index):
+        at = index // 2
+        return index % 2 * chips + at % planes * per + at // planes
+
     local_row = lax.broadcasted_iota(jnp.int32, (span, 1), 0)
     owner = lax.shift_right_logical(local_row * 43691, 17)
-    place = owner * (wrows * columns) + (local_row - owner * wrows) * columns
+    place = arrival(owner) * (wrows * columns) + (local_row - owner * wrows) * columns
     lane = lax.broadcasted_iota(jnp.int32, (span, width), 1)
     for c in range(columns):
         order[c * span:(c + 1) * span] = jnp.where(lane == place + c, 1.0, 0.0).astype(jnp.bfloat16)
     pl.semaphore_wait(barrier, seqs + columns - 2)
 
     def plane_copy(k):
-        other = (column + k) % columns
-        return send(wsend.at[other % ring], wplane.at[column], p_send.at[k], p_recv.at[column], other, me)
-
-    def plane_start(k, _):
+        goal = (x + k) % ring
+        return send(
+            wsend.at[goal], wplane.at[column], p_send.at[k], p_recv.at[column], z % planes * ring + goal, me)
+
+    for k in range(1, ring):
         plane_copy(k).start()
-        return 0
-
-    lax.fori_loop(1, columns, plane_start, 0)
-    plane_own = pltpu.make_async_copy(wsend.at[x], wplane.at[column], p_recv.at[column])
-    plane_own.start()
+
+    @pl.when(z % planes != y)
+    def _():
+        plane_copy(0).start()
+
+    @pl.when(z % planes == y)
+    def _():
+        pltpu.make_async_copy(wsend.at[x], wplane.at[column], p_recv.at[column]).start()
 
     def slot(offset, part):
         return ((x + offset + ring) % ring) * part_dev + part
@@ -111,6 +130,8 @@
         ref = mod_all.at[slot(offset, part)]
         return send(ref, ref, x_send.at[leg, part], x_recv.at[leg, part], target, me)
 
+    for copy in inputs:
+        copy.wait()
     mod_row = mod_ref[pl.ds(step_ref[0], 1), :]
     shift, scale = mod_row[:, 0:width], mod_row[:, width:2 * width]
     for part in range(part_dev):
@@ -158,18 +179,18 @@
     def q_own(part, head):
         return pltpu.make_async_copy(q_out.at[part, head], q_all.at[me], q_recv.at[me])
 
-    def project(offset):
+    def project_kv(offset, group):
         base = slot(offset, 0)
-        states = mod_all[pl.ds(base, part_dev)].reshape(part_dev * rows, width)
-        for group in range(cols // 2):
-            lanes = slice((cols // 2) * 128 + group * 256, (cols // 2) * 128 + (group + 1) * 256)
-            kv = jnp.dot(states, wbuf[:, lanes], preferred_element_type=jnp.float32)
-            for part in range(part_dev):
-                for side in range(2):
-                    piece = kv[part * rows:(part + 1) * rows, side * 128:(side + 1) * 128]
-                    kv_out[base + part, 2 * group + side] = piece.astype(jnp.bfloat16)
-                    post(kv_copy, kv_own, base + part, 2 * group + side)
-        query = jnp.dot(states, wbuf[:, 0:(cols // 2) * 128], preferred_element_type=jnp.float32)
+        kv = jnp.dot(states_of(offset), wbuf[group], preferred_element_type=jnp.float32)
+        for part in range(part_dev):
+            for side in range(2):
+                piece = kv[part * rows:(part + 1) * rows, side * 128:(side + 1) * 128]
+                kv_out[base + part, 2 * group + side] = piece.astype(jnp.bfloat16)
+                post(kv_copy, kv_own, base + part, 2 * group + side)
+
+    def project_q(offset):
+        base = slot(offset, 0)
+        query = jnp.dot(states_of(offset), wbuf[PIECES - 1], preferred_element_type=jnp.float32)
         low = low_lanes((half, 128))
         for part in range(part_dev):
             for group in range(cols // 2):
@@ -179,84 +200,111 @@
                 q_out[base + part, 2 * group] = jnp.where(low, upper, swap_halves(lower)).astype(jnp.bfloat16)
                 q_out[base + part, 2 * group + 1] = jnp.where(low, swap_halves(upper), lower).astype(jnp.bfloat16)
 
-    def plane_wait(k, _):
-        src = (column + k) % columns
-        send(wsend.at[0], wplane.at[src], p_send.at[k], p_recv.at[src], column, me).wait_recv()
-        return 0
-
-    lax.fori_loop(0, columns, plane_wait, 0)
+    def weight_place(group):
+        if group < cols // 2:
+            return PIECES - 1, slice(group * 128, (group + 1) * 128)
+        head = group - cols // 2
+        return head // 2, slice(head % 2 * 128, (head % 2 + 1) * 128)
+
     block_rows = wrows * columns
 
-    def weight_rows(index):
-        return wbuf.at[pl.ds(pl.multiple_of(index * block_rows, block_rows), block_rows)]
-
-    base_row = pl.multiple_of(me * block_rows, block_rows)
-    for group in range(3 * cols // 2):
-        for i in range(wrows):
-            wbuf[pl.ds(base_row + i * columns, columns), group * 128:(group + 1) * 128] = (
-                wplane[:, i, group, :].astype(jnp.bfloat16))
-    chips = seqs // 2
-    sibling = me + 1 - 2 * (me % 2)
-
-    def around(hops):
-        return (me + 2 * hops + seqs) % seqs
-
-    def weight_copy(index, leg, hop, target):
-        return send(weight_rows(index), weight_rows(index), w_send.at[leg, hop], w_recv.at[index], column, target)
-
-    def weight_wait(index):
-        weight_copy(index, 0, 0, me).wait_recv()
-
-    reach = (chips // 2, chips - 1 - chips // 2)
-    started = []
-
-    def weight_start(*args):
-        copy = weight_copy(*args)
-        copy.start()
-        started.append(copy)
-
-    weight_start(me, 0, 0, around(1))
-    weight_start(me, 1, 0, around(-1))
-    weight_start(me, 2, 0, sibling)
-    for hop in range(1, reach[0] + 1):
-        index = around(-hop)
-        weight_wait(index)
-        if hop < reach[0]:
-            weight_start(index, 0, hop, around(1))
-        weight_start(index, 2, hop, sibling)
-        if hop <= reach[1]:
-            index = around(hop)
-            weight_wait(index)
-            if hop < reach[1]:
-                weight_start(index, 1, hop, around(-1))
-            weight_start(index, 3, hop, sibling)
-        if hop == FORWARD_AT:
-            ring_copy(-1, 0, 0, right).wait_recv()
-            ring_copy(-1, 0, 2, right).start()
-            ring_copy(1, 1, 1, left).wait_recv()
-            ring_copy(1, 1, 2, left).start()
-
-    def sibling_wait(k, _):
-        weight_wait((sibling + 2 * k) % seqs)
-        return 0
-
-    lax.fori_loop(0, chips, sibling_wait, 0)
-    project(0)
+    def weight_ref_of(piece, start, count):
+        return wbuf.at[piece, pl.ds(pl.multiple_of(start * block_rows, block_rows), count * block_rows)]
+
+    def z_copy(piece, hops):
+        ref = weight_ref_of(piece, arrival(me), 1)
+        return send(ref, ref, z_send.at[piece, hops], z_recv.at[piece, z // planes], column, (me + 2 * hops) % seqs)
+
+    def y_copy(piece, hops):
+        ref = weight_ref_of(piece, core * chips + y * per, per)
+        goal = (column + hops * ring) % columns
+        return send(ref, ref, y_send.at[piece, hops], y_recv.at[piece, planes - hops], goal, me)
+
+    def core_copy(piece):
+        ref = weight_ref_of(piece, core * chips, chips)
+        return send(ref, ref, b_send.at[piece], b_recv.at[piece], column, me + 1 - 2 * core)
+
+    @pl.when(z % planes == y)
+    def _():
+        def plane_wait(k, _):
+            src = (column + k) % columns
+            send(wsend.at[0], wplane.at[src], p_send.at[0], p_recv.at[src], column, me).wait_recv()
+            return 0
+
+        lax.fori_loop(0, columns, plane_wait, 0)
+        base_row = pl.multiple_of(arrival(me) * block_rows, block_rows)
+        for group in range(3 * cols // 2):
+            piece, lanes = weight_place(group)
+            for i in range(wrows):
+                wbuf[piece, pl.ds(base_row + i * columns, columns), lanes] = (
+                    wplane[:, i, group, :].astype(jnp.bfloat16))
+        for piece in range(PIECES):
+            def z_start(hops, _):
+                z_copy(piece, hops).start()
+                return 0
+
+            lax.fori_loop(1, chips, z_start, 0)
+
+    def z_pass(piece):
+        for m in range(per):
+            source = m * planes + y
+
+            @pl.when(source != z)
+            def _():
+                ref = weight_ref_of(piece, core * chips + y * per + m, 1)
+                send(ref, ref, z_send.at[piece, 0], z_recv.at[piece, m], column, me).wait_recv()
+
+        for hops in range(1, planes):
+            y_copy(piece, hops).start()
+
+    def y_pass(piece):
+        for hops in range(1, planes):
+            ref = weight_ref_of(piece, core * chips + (y + hops) % planes * per, per)
+            send(ref, ref, y_send.at[piece, 0], y_recv.at[piece, hops], column, me).wait_recv()
+        core_copy(piece).start()
+
+    def core_wait(piece):
+        ref = weight_ref_of(piece, (1 - core) * chips, chips)
+        send(ref, ref, b_send.at[piece], b_recv.at[piece], column, me).wait_recv()
+
+    def states_of(offset):
+        return mod_all[pl.ds(slot(offset, 0), part_dev)].reshape(part_dev * rows, width)
+
+    z_pass(0)
+    z_pass(1)
+    y_pass(0)
+    z_pass(2)
+    ring_copy(-1, 0, 0, right).wait_recv()
+    ring_copy(-1, 0, 2, right).start()
+    ring_copy(1, 1, 1, left).wait_recv()
+    ring_copy(1, 1, 2, left).start()
+    core_wait(0)
+    project_kv(0, 0)
+    y_pass(1)
+    y_pass(2)
+    core_wait(1)
+    project_kv(0, 1)
     ring_copy(-1, 1, 0, right).wait_recv()
     ring_copy(1, 0, 1, left).wait_recv()
-    project(-1)
-    project(1)
+    for offset in (-1, 1):
+        for group in range(cols // 2):
+            project_kv(offset, group)
     for part in range(part_dev):
         ring_copy(2, part, 2, right).wait_recv()
-    project(2)
+    for group in range(cols // 2):
+        project_kv(2, group)
+    core_wait(PIECES - 1)
     for offset in (0, -1, 1, 2):
+        project_q(offset)
         for part in range(part_dev):
             for head in range(cols):
                 post(q_copy, q_own, slot(offset, part), head)
 
     text_copy.wait()
     kv_all[image:image + TEXT_PAD] = jnp.zeros((TEXT_PAD, 128), jnp.bfloat16)
-    kv_all[image:image + txt] = text_buf[...]
+    heads = lax.broadcasted_iota(jnp.int32, (txt, HEADS, 128), 1)
+    mine = jnp.where(heads == x * cols + me // particles, text_buf[...].astype(jnp.float32), 0.0)
+    kv_all[image:image + txt] = jnp.sum(mine, axis=1).astype(jnp.bfloat16)
 
     def kv_wait(k, _):
         src = (me + k) % seqs
@@ -367,13 +415,25 @@
     ring_copy(-1, 0, 2, right).wait_send()
     ring_copy(1, 1, 2, left).wait_send()
 
-    def plane_sent(k, _):
+    for k in range(1, ring):
         plane_copy(k).wait_send()
-        return 0
-
-    lax.fori_loop(1, columns, plane_sent, 0)
-    for copy in started:
-        copy.wait_send()
+
+    @pl.when(z % planes != y)
+    def _():
+        plane_copy(0).wait_send()
+
+    for piece in range(PIECES):
+        @pl.when(z % planes == y)
+        def _():
+            def z_sent(hops, _):
+                z_copy(piece, hops).wait_send()
+                return 0
+
+            lax.fori_loop(1, chips, z_sent, 0)
+
+        for hops in range(1, planes):
+            y_copy(piece, hops).wait_send()
+        core_copy(piece).wait_send()
 
     def item_sent(k, _):
         target = (me + k) % seqs
@@ -402,40 +462,43 @@
     joint = seqs * rows + TEXT_PAD
     bf16, f32 = jnp.bfloat16, jnp.float32
     vmem, dma = pltpu.VMEM, pltpu.SemaphoreType.DMA
+    any_spec = pl.BlockSpec(memory_space=pl.ANY)
     smem_spec, vmem_spec = pl.BlockSpec(memory_space=pltpu.SMEM), pl.BlockSpec(memory_space=pltpu.VMEM)
     return pl.pallas_call(
         functools.partial(block_kernel, cols, ring, columns, seqs, txt),
         out_shape=jax.ShapeDtypeStruct((part_dev, rows, HEADS * HD), bf16),
-        in_specs=[smem_spec, smem_spec, vmem_spec, vmem_spec, vmem_spec, pl.BlockSpec(memory_space=pl.ANY)],
+        in_specs=[smem_spec, any_spec, any_spec, any_spec, vmem_spec, any_spec],
         out_specs=vmem_spec,
         scratch_shapes=[
+            pltpu.SMEM(ancestors.shape, jnp.int32), vmem(latents.shape, bf16), vmem(mod_table.shape, f32), dma((3,)),
             vmem((PER_PROMPT, rows, width), bf16),
             vmem((width, width), bf16),
             vmem((ring, wrows, ROW_PAD, 128), f32),
             vmem((columns, wrows, ROW_PAD, 128), f32),
-            vmem((width, 3 * cols * HD), bf16),
+            vmem((PIECES, width, cols * HD), bf16),
             vmem((PER_PROMPT, cols, rows, 128), bf16),
             vmem((PER_PROMPT, cols, rows // 2, 128), bf16),
             vmem((joint, 128), bf16),
             vmem((HD, joint), bf16),
             vmem((seqs, rows // 2, 128), bf16),
-            vmem((txt, 128), bf16),
+            vmem((txt, HEADS, 128), bf16),
             vmem((joint, SLICES * rows), f32),
             vmem((joint, SLICES * rows), bf16),
             vmem((seqs, rows // 2, 128), bf16),
             vmem((seqs, rows // 2, 128), bf16),
             vmem((ring, part_dev, rows, cols * HD), bf16),
             dma((3, part_dev)), dma((3, part_dev)),
-            dma((columns,)), dma((columns,)),
-            dma((4, seqs // 4 + 1)), dma((seqs,)), dma,
+            dma((ring,)), dma((columns,)),
+            dma((PIECES, seqs // 2)), dma((PIECES, seqs // 2 * ring // columns)),
+            dma((PIECES, columns // ring)), dma((PIECES, columns // ring)), dma((PIECES,)), dma((PIECES,)), dma,
             dma((items,)), dma((items,)), dma((items,)), dma((items,)), dma((items,)), dma((items,)),
             dma((ring,)), dma((ring,)),
         ],
         compiler_params=pltpu.CompilerParams(
-            collective_id=0, has_side_effects=True, vmem_limit_bytes=52 * 2**20),
+            collective_id=0, has_side_effects=True, vmem_limit_bytes=60 * 2**20),
         cost_estimate=pl.CostEstimate(flops=7 * 10**9, bytes_accessed=4 * 10**6, transcendentals=18 * 10**6),
         name="steered_block",
-    )(ancestors, step_index, latents, mod_table, qkv_weight, text_kv)
+    )(step_index, ancestors, latents, mod_table, qkv_weight, text_kv.transpose(1, 0, 2))
 
 
 def solution(mesh):

time: 173 us -> 164 us (0.948)
  Pallas kernels: 167 us -> 161 us
  local copies, waits for them, and re-layouts: 5.66 us -> 1.87 us
    pallas_call x1, Pallas kernels: 167 us -> 161 us  [local(): pl.pallas_call(functools.partial(block_kernel, cols, ring, columns, seqs,...]
    unnamed x10 -> x1, local copies, waits for them, and re-layouts: 5.66 us -> 1.87 us
where the time goes in v3:
time: 164 us
  Pallas kernels  161 us (98%)
  local copies, waits for them, and re-layouts  1.87 us (1%)
    pallas_call x1, Pallas kernels, local(): pl.pallas_call(functools.partial(block_kernel, cols, ring, columns, seqs,...  161 us

profile of v3, /device:TPU:1, one launch (start us, length us, event | category | flops | bytes accessed | tf_op | source)
XLA Modules:
  0.0 163.6 jit_solution(14587330140406727610)
XLA Ops:
  0.7 161.1 %steered_block.1 = bf16[2,128,1024]{2,1,0:T(8,128)(2,1)} custom-call(s32[1]{0:T(128)S(6)} %copy.8.step_ref, s32[32]{0:T(128)} %anc_any.1, bf16[2,128,1536]{2,1,0:T(8,128)(2,1)} %lat_any.1, f32[28,3072]{1,0:T(8,128)} %mod_any.1, bf16[3,3072]{1,0:T(4,128)(2,1)} %weight_ref.1, bf16[154,64,128]{2,1,0:T(8,128)(2,1)} %bitcast.1), custom_call_target="tpu_custom_call" | custom-call | flops 7000000000 | bytes 4000000 | tf_op jit(solution)/shard_map/steered_block/pallas_call | solution.py:467
  161.8 1.9 %copy.9 = bf16[2,128,1024]{2,1,0:T(8,128)(2,1)} copy(bf16[2,128,1024]{2,1,0:T(8,128)(2,1)} %steered_block.1) | data formatting | bytes 1048576

commit v4 on v3

--- a/solution.py
+++ b/solution.py
@@ -147,7 +147,14 @@
         ring_copy(0, part_dev - 1 - part, 1, left).start()
 
     def item_seq(part, head):
-        return head * particles + part
+        position, which = part // 2, part % 2
+        chip = which * (chips // 2) + head % 2 * (chips // 4) + head // 2 * 2 + position // 2
+        return chip * 2 + position % 2
+
+    def item_of(target):
+        chip = target // 2
+        head = chip // (chips // 4) % 2 + chip // 2 % 2 * 2
+        return (chip % 2 * 2 + target % 2) * 2 + chip // (chips // 2), head
 
     def kv_copy(part, head):
         return send(
@@ -303,7 +310,7 @@
     text_copy.wait()
     kv_all[image:image + TEXT_PAD] = jnp.zeros((TEXT_PAD, 128), jnp.bfloat16)
     heads = lax.broadcasted_iota(jnp.int32, (txt, HEADS, 128), 1)
-    mine = jnp.where(heads == x * cols + me // particles, text_buf[...].astype(jnp.float32), 0.0)
+    mine = jnp.where(heads == x * cols + item_of(me)[1], text_buf[...].astype(jnp.float32), 0.0)
     kv_all[image:image + txt] = jnp.sum(mine, axis=1).astype(jnp.bfloat16)
 
     def kv_wait(k, _):
@@ -334,7 +341,8 @@
         return result
 
     def attend(step, _):
-        base = (me // SLICES + step) % (seqs // SLICES) * SLICES
+        groups = seqs // SLICES
+        base = (me // SLICES + groups + step * (1 - 2 * core)) % groups * SLICES
         queries = []
         lower_lanes = low_lanes((half, 128))
         for side in range(SLICES):
@@ -397,8 +405,8 @@
         for part in range(part_dev):
             source = anc_ref[(first + goal) * part_dev + part] % particles
             for group in range(cols // 2):
-                even = o_all[2 * group * particles + source].astype(jnp.float32)
-                odd = o_all[(2 * group + 1) * particles + source].astype(jnp.float32)
+                even = o_all[item_seq(source, 2 * group)].astype(jnp.float32)
+                odd = o_all[item_seq(source, 2 * group + 1)].astype(jnp.float32)
                 lanes = slice(group * 128, (group + 1) * 128)
                 chosen[k, part, 0:half, lanes] = jnp.where(low, even, swap_halves(odd)).astype(jnp.bfloat16)
                 chosen[k, part, half:rows, lanes] = jnp.where(low, swap_halves(even), odd).astype(jnp.bfloat16)
@@ -437,7 +445,7 @@
 
     def item_sent(k, _):
         target = (me + k) % seqs
-        part, head = target % particles, target // particles
+        part, head = item_of(target)
         kv_copy(part, head).wait_send()
         q_copy(part, head).wait_send()
         o_copy(target, target).wait_send()

time: 164 us -> 160 us (0.976)
  Pallas kernels: 161 us -> 157 us
    pallas_call x1, Pallas kernels: 161 us -> 157 us  [local(): pl.pallas_call(functools.partial(block_kernel, cols, ring, columns, seqs,...]
where the time goes in v4:
time: 160 us
  Pallas kernels  157 us (98%)
  local copies, waits for them, and re-layouts  1.87 us (1%)
    pallas_call x1, Pallas kernels, local(): pl.pallas_call(functools.partial(block_kernel, cols, ring, columns, seqs,...  157 us

profile of v4, /device:TPU:1, one launch (start us, length us, event | category | flops | bytes accessed | tf_op | source)
XLA Modules:
  0.0 159.5 jit_solution(11232091730952177892)
XLA Ops:
  0.7 157.0 %steered_block.1 = bf16[2,128,1024]{2,1,0:T(8,128)(2,1)} custom-call(s32[1]{0:T(128)S(6)} %copy.8.step_ref, s32[32]{0:T(128)} %anc_any.1, bf16[2,128,1536]{2,1,0:T(8,128)(2,1)} %lat_any.1, f32[28,3072]{1,0:T(8,128)} %mod_any.1, bf16[3,3072]{1,0:T(4,128)(2,1)} %weight_ref.1, bf16[154,64,128]{2,1,0:T(8,128)(2,1)} %bitcast.1), custom_call_target="tpu_custom_call" | custom-call | flops 7000000000 | bytes 4000000 | tf_op jit(solution)/shard_map/steered_block/pallas_call | solution.py:475
  157.6 1.9 %copy.9 = bf16[2,128,1024]{2,1,0:T(8,128)(2,1)} copy(bf16[2,128,1024]{2,1,0:T(8,128)(2,1)} %steered_block.1) | data formatting | bytes 1048576
